TPU v7x, 512 devices: a whole 4x8x8 slice. The times are simulated.
512 devices in a mesh: tile: 64 (over x, y, core), fblk: 8 (over z).
Axes of the slice: x: 4, y: 8, z: 8, core: 2. Of those that a mesh axis runs over, the one named last changes fastest.
Arguments:
- planes: float32 [512, 1024, 128], P(('fblk', 'tile')), may hold values from -40000 to 40000
- widths: int32 [4], replicated, may hold values from 1 to 8, as said below
Outputs:
- peak_maps: float32 [4, 1024, 128], P(None, 'tile')
Inputs may be any that keep to these rules, and one draw needn't show every extreme that they name: `widths`: some kernel has width 8 in every draw.
All inputs are finite; a program needn't handle non-finite values.
Results may differ from a plain program's by a relative error of at most 0.0001.
Values sent between devices are 32-bit elements; how exact they have to be, the bound alone decides.
No kernel may reach another device: no remote copies, remote signals or barrier semaphores. Data moves between devices by JAX's collectives and lax.ppermute only.
A program may use at most 64 MiB of HBM per device.

v0:
```python
import jax
import jax.numpy as jnp
from jax import lax
from jax.sharding import PartitionSpec as P

KERNELS = 4
RAD = 8
MAXW = 8
SIGMAS = (1.0, 1.6, 2.3, 3.2)
EPSILON = 1e-06


def shifted(block, axis, distance):
    devices = range(lax.axis_size(axis))
    route = [(i - distance, i) for i in devices if i - distance in devices]
    return lax.ppermute(block, axis, route)


def with_halo(value, sides, width):
    for axis, dim in sides:
        peers, length = (lax.axis_size(axis), value.shape[dim])
        up = [(i, (i + 1) % peers) for i in range(peers - 1)]
        down = [(j, i) for i, j in up]
        last = lax.slice_in_dim(value, length - width, length, axis=dim)
        leading = lax.slice_in_dim(value, 0, width, axis=dim)
        before = lax.ppermute(last, axis, up)
        after = lax.ppermute(leading, axis, down)
        value = jnp.concatenate([before, value, after], axis=dim)
    return value


def kernel_for(sigma):
    offsets = jnp.arange(2 * RAD + 1).astype(jnp.float32) - RAD
    values = jnp.exp(-offsets * offsets / (2.0 * sigma * sigma))
    return values / jnp.sum(values)


def pad_along(values, along):
    margins = [(0, 0)] * values.ndim
    margins[along] = (RAD, RAD)
    return jnp.pad(values, margins)


def filter_along(padded, kernel, along):
    length = padded.shape[along] - 2 * RAD
    summed = jnp.zeros(lax.slice_in_dim(padded, 0, length, axis=along).shape, jnp.float32)
    for offset in range(2 * RAD + 1):
        summed = summed + kernel[offset] * lax.slice_in_dim(
            padded, offset, offset + length, axis=along
        )
    return summed


def boxcar(extended, width, channels):
    scale = 1.0 / jnp.sqrt(width.astype(jnp.float32))
    summed = jnp.zeros((channels,) + extended.shape[1:], jnp.float32)
    for offset in range(MAXW):
        weight = jnp.where(offset < width, 1.0, 0.0).astype(jnp.float32) * scale
        summed = summed + weight * extended[offset : offset + channels]
    return summed


def channel_peak(smoothed, sum_squares, cells):
    rms_values = jnp.sqrt(sum_squares / cells + EPSILON)
    return jnp.max(smoothed / rms_values[:, None, None], axis=0)


def body(planes, widths):
    relaid = lax.all_to_all(planes, "tile", split_axis=1, concat_axis=0, tiled=True)
    channels = relaid.shape[0]
    cells = relaid.shape[1] * lax.axis_size("tile") * relaid.shape[2]
    band_edge = shifted(relaid[: MAXW - 1], "fblk", -1)
    extended = jnp.concatenate([relaid, band_edge], axis=0)
    peak_list = []
    for kernel_id in range(KERNELS):
        kernel = kernel_for(SIGMAS[kernel_id])
        spectral = boxcar(extended, widths[kernel_id], channels)
        horizontal = filter_along(pad_along(spectral, 2), kernel, 2)
        bordered = with_halo(horizontal, (("tile", 1),), RAD)
        smoothed = filter_along(bordered, kernel, 1)
        sum_squares = lax.psum(jnp.sum(smoothed * smoothed, axis=(1, 2)), "tile")
        peak_list.append(channel_peak(smoothed, sum_squares, cells))
    return lax.pmax(jnp.stack(peak_list), "fblk")


def solution(mesh):
    placed = (P(("fblk", "tile"), None, None), P())
    return jax.shard_map(
        body, mesh=mesh, in_specs=placed, out_specs=P(None, "tile", None), check_vma=False
    )
```

profile of v0, /device:TPU:64, one launch (start us, length us, event | category | flops | bytes accessed | tf_op | source)
XLA Modules:
  0.0 334.0 jit_solution(15228907142696872255)
XLA Ops:
  0.0 10.7 %all-to-all-start = ((f32[1,1024,128]{2,0,1:T(1,128)}), f32[1,1024,128]{2,0,1:T(1,128)S(1)}, u32[]{:S(2)}, u32[]{:S(2)}) async-start(f32[1,1024,128]{2,0,1:T(1,128)} %bitcast.111), calls=%async_computation | async-start | bytes 1048576 | tf_op jit(solution)/shard_map/all_to_all | solution.py:69
  39.6 0.7 fusion.340
  40.3 0.7 fusion.339
  41.8 1.9 collective-permute-start
  43.7 0.7 fusion.336
  44.4 3.8 %collective-permute-done = f32[7,16,128]{2,1,0:T(8,128)S(1)} collective-permute-done((f32[7,16,128]{2,1,0:T(8,128)S(1)}, f32[7,16,128]{2,1,0:T(8,128)S(1)}, u32[]{:S(2)}, u32[]{:S(2)}) %collective-permute-start) | collective-permute-done | bytes 57376 | tf_op jit(solution)/shard_map/ppermute | solution.py:16
  48.9 12.7 %fusion.230 = f32[64,16,128]{2,1,0:T(8,128)S(1)} fusion(f32[64,16,128]{2,1,0:T(8,128)S(1)} %multiply_add_fusion.2, f32[]{:T(128)} %bitcast.53, f32[]{:T(128)} %bitcast.52, f32[]{:T(128)} %bitcast.51, f32[]{:T(128)} %bitcast.50, f32[]{:T(128)} %bitcast.49, f32[]{:T(128)} %bitcast.48, f32[]{:T(128)} %bitcast.47, f32[]{:T(128)} %bitcast.46, f32[]{:T(128)} %bitcast.45, ...), kind=kLoop, calls=%fused_computation.418 | loop fusion | flops 4325376 | bytes 1048644 | tf_op jit(solution)/shard_map/add | solution.py:48
  61.6 1.3 collective-permute-start.3
  62.9 1.3 collective-permute-start.4
  64.5 12.8 %fusion.294 = f32[64,16,128]{2,1,0:T(8,128)S(1)} fusion(f32[64,16,128]{2,1,0:T(8,128)S(1)} %multiply_add_fusion, f32[]{:T(128)} %bitcast.105, f32[]{:T(128)} %bitcast.104, f32[]{:T(128)} %bitcast.103, f32[]{:T(128)} %bitcast.102, f32[]{:T(128)} %bitcast.101, f32[]{:T(128)} %bitcast.100, f32[]{:T(128)} %bitcast.99, f32[]{:T(128)} %bitcast.98, f32[]{:T(128)} %bitcast.97, ...), kind=kLoop, calls=%fused_computation.482 | loop fusion | flops 4325376 | bytes 1048644 | tf_op jit(solution)/shard_map/add | solution.py:48
  77.3 4.9 %collective-permute-start.7 = (f32[64,8,128]{2,1,0:T(8,128)S(1)}, f32[64,8,128]{2,1,0:T(8,128)S(1)}, u32[]{:S(2)}, u32[]{:S(2)}) collective-permute-start(f32[64,8,128]{2,1,0:T(8,128)S(1)} %get-tuple-element.30), channel_id=1, source_target_pairs={{0,8},{8,16},{16,24},{24,32},{32,40},{40,48},{48,56},{56,64},{64,7... | collective-permute-start | bytes 786440 | tf_op jit(solution)/shard_map/ppermute | solution.py:26
  82.2 1.3 collective-permute-start.8
  83.8 12.9 %fusion.262 = f32[64,16,128]{2,1,0:T(8,128)S(1)} fusion(f32[64,16,128]{2,1,0:T(8,128)S(1)} %multiply_add_fusion.1, f32[]{:T(128)} %bitcast.79, f32[]{:T(128)} %bitcast.78, f32[]{:T(128)} %bitcast.77, f32[]{:T(128)} %bitcast.76, f32[]{:T(128)} %bitcast.75, f32[]{:T(128)} %bitcast.74, f32[]{:T(128)} %bitcast.73, f32[]{:T(128)} %bitcast.72, f32[]{:T(128)} %bitcast.71, ...), kind=kLoop, calls=%fused_computation.450 | loop fusion | flops 4325376 | bytes 1048644 | tf_op jit(solution)/shard_map/add | solution.py:48
  96.8 4.3 %collective-permute-start.5 = (f32[64,8,128]{2,1,0:T(8,128)S(1)}, f32[64,8,128]{2,1,0:T(8,128)S(1)}, u32[]{:S(2)}, u32[]{:S(2)}) collective-permute-start(f32[64,8,128]{2,1,0:T(8,128)S(1)} %get-tuple-element.28), channel_id=1, source_target_pairs={{0,8},{8,16},{16,24},{24,32},{32,40},{40,48},{48,56},{56,64},{64,7... | collective-permute-start | bytes 786440 | tf_op jit(solution)/shard_map/ppermute | solution.py:26
  101.0 12.8 %fusion.198 = f32[64,16,128]{2,1,0:T(8,128)S(1)} fusion(f32[64,16,128]{2,1,0:T(8,128)S(1)} %get-tuple-element.11, f32[]{:T(128)} %bitcast.27, f32[]{:T(128)} %bitcast.26, f32[]{:T(128)} %bitcast.25, f32[]{:T(128)} %bitcast.24, f32[]{:T(128)} %bitcast.23, f32[]{:T(128)} %bitcast.22, f32[]{:T(128)} %bitcast.21, f32[]{:T(128)} %bitcast.20, f32[]{:T(128)} %bitcast.19, ...), kind=kLoop, calls=%fused_computation.386 | loop fusion | flops 4325376 | bytes 1048644 | tf_op jit(solution)/shard_map/add | solution.py:48
  113.9 1.3 collective-permute-start.6
  115.2 4.4 %collective-permute-start.1 = (f32[64,8,128]{2,1,0:T(8,128)S(1)}, f32[64,8,128]{2,1,0:T(8,128)S(1)}, u32[]{:S(2)}, u32[]{:S(2)}) collective-permute-start(f32[64,8,128]{2,1,0:T(8,128)S(1)} %get-tuple-element.24), channel_id=1, source_target_pairs={{0,8},{8,16},{16,24},{24,32},{32,40},{40,48},{48,56},{56,64},{64,7... | collective-permute-start | bytes 786440 | tf_op jit(solution)/shard_map/ppermute | solution.py:26
  119.7 12.5 %multiply_reduce_fusion.2 = (f32[64]{0:T(128)S(1)}, f32[64,16,128]{2,1,0:T(8,128)S(1)}) fusion(f32[64,8,128]{2,1,0:T(8,128)S(1)} %collective-permute-done.4, f32[64,16,128]{2,1,0:T(8,128)S(1)} %fusion.230, f32[]{:T(128)} %bitcast.53, f32[]{:T(128)} %bitcast.52, f32[]{:T(128)} %bitcast.51, f32[]{:T(128)} %bitcast.50, f32[]{:T(128)} %bitcast.49, f32[]{:T(128)} %bitcast.48, ...), kind=kLoop, calls=%fused_computation.519 | loop fusion | flops 6684608 | bytes 1573188 | tf_op jit(solution)/shard_map/reduce_sum | solution.py:81
  132.2 1.3 collective-permute-start.2
  133.5 12.6 %multiply_reduce_fusion = (f32[64]{0:T(128)S(1)}, f32[64,16,128]{2,1,0:T(8,128)S(1)}) fusion(f32[64,8,128]{2,1,0:T(8,128)S(1)} %collective-permute-done.8, f32[64,16,128]{2,1,0:T(8,128)S(1)} %fusion.294, f32[]{:T(128)} %bitcast.105, f32[]{:T(128)} %bitcast.104, f32[]{:T(128)} %bitcast.103, f32[]{:T(128)} %bitcast.102, f32[]{:T(128)} %bitcast.101, ...), kind=kLoop, calls=%fused_computation.515 | loop fusion | flops 6684608 | bytes 1573188 | tf_op jit(solution)/shard_map/reduce_sum | solution.py:81
  146.1 12.7 %multiply_reduce_fusion.1 = (f32[64]{0:T(128)S(1)}, f32[64,16,128]{2,1,0:T(8,128)S(1)}) fusion(f32[64,8,128]{2,1,0:T(8,128)S(1)} %collective-permute-done.6, f32[64,16,128]{2,1,0:T(8,128)S(1)} %fusion.262, f32[]{:T(128)} %bitcast.79, f32[]{:T(128)} %bitcast.78, f32[]{:T(128)} %bitcast.77, f32[]{:T(128)} %bitcast.76, f32[]{:T(128)} %bitcast.75, f32[]{:T(128)} %bitcast.74, ...), kind=kLoop, calls=%fused_computation.517 | loop fusion | flops 6684608 | bytes 1573188 | tf_op jit(solution)/shard_map/reduce_sum | solution.py:81
  158.8 12.6 %multiply_reduce_fusion.3 = (f32[64]{0:T(128)S(1)}, f32[64,16,128]{2,1,0:T(8,128)S(1)}) fusion(f32[64,8,128]{2,1,0:T(8,128)S(1)} %collective-permute-done.2, f32[64,16,128]{2,1,0:T(8,128)S(1)} %fusion.198, f32[]{:T(128)} %bitcast.27, f32[]{:T(128)} %bitcast.26, f32[]{:T(128)} %bitcast.25, f32[]{:T(128)} %bitcast.24, f32[]{:T(128)} %bitcast.23, f32[]{:T(128)} %bitcast.22, ...), kind=kLoop, calls=%fused_computation.521 | loop fusion | flops 6684608 | bytes 1573188 | tf_op jit(solution)/shard_map/reduce_sum | solution.py:81
  171.5 130.0 %all-reduce.4 = (f32[64]{0:T(128)S(1)}, f32[64]{0:T(128)S(1)}, f32[64]{0:T(128)S(1)}, f32[64]{0:T(128)S(1)}) all-reduce(f32[64]{0:T(128)S(1)} %get-tuple-element.22, f32[64]{0:T(128)S(1)} %get-tuple-element.20, f32[64]{0:T(128)S(1)} %get-tuple-element.18, f32[64]{0:T(128)S(1)} %get-tuple-element.9), channel_id=1, replica_groups=mesh['tile'=64,'fblk'=8] {'tile'}, use_global_device_ids=true, to_apply=%region_14.15 | all-reduce | flops 256 | bytes 2048 | tf_op jit(solution)/shard_map/psum | solution.py:81
  302.1 31.9 %pmax.7 = f32[4,16,128]{2,1,0:T(8,128)} all-reduce(f32[4,16,128]{2,1,0:T(8,128)S(1)} %pad_maximum_fusion.9), channel_id=1, replica_groups=mesh['tile'=64,'fblk'=8] {'fblk'}, use_global_device_ids=true, to_apply=%region_16.17 | all-reduce | flops 8192 | bytes 65536 | tf_op jit(solution)/shard_map/pmax | solution.py:83
  (37 shorter events, 8.5 us)
Async XLA Ops:
  0.0 10.7 %copy-start = (s32[4]{0:T(128)S(1)}, s32[4]{0:T(128)}, u32[]{:S(2)}) copy-start(s32[4]{0:T(128)} %param.3) | copy-start | bytes 52
  0.0 41.8 %all-to-all-start = ((f32[1,1024,128]{2,0,1:T(1,128)}), f32[1,1024,128]{2,0,1:T(1,128)S(1)}, u32[]{:S(2)}, u32[]{:S(2)}) async-start(f32[1,1024,128]{2,0,1:T(1,128)} %bitcast.111), calls=%async_computation | async-start | bytes 1048576 | tf_op jit(solution)/shard_map/all_to_all | solution.py:69
  41.8 6.4 %collective-permute-start = (f32[7,16,128]{2,1,0:T(8,128)S(1)}, f32[7,16,128]{2,1,0:T(8,128)S(1)}, u32[]{:S(2)}, u32[]{:S(2)}) collective-permute-start(f32[7,16,128]{2,1,0:T(8,128)S(1)} %bitcast.112), channel_id=1, source_target_pairs={{1,0},{2,1},{3,2},{4,3},{5,4},{6,5},{7,6},{9,8},{10,9},{11,10},{12... | collective-permute-start | bytes 172040 | tf_op jit(solution)/shard_map/ppermute | solution.py:16
  61.6 52.3 %collective-permute-start.3 = (f32[64,8,128]{2,1,0:T(8,128)S(1)}, f32[64,8,128]{2,1,0:T(8,128)S(1)}, u32[]{:S(2)}, u32[]{:S(2)}) collective-permute-start(f32[64,8,128]{2,1,0:T(8,128)S(1)} %get-tuple-element.26), channel_id=1, source_target_pairs={{0,8},{8,16},{16,24},{24,32},{32,40},{40,48},{48,56},{56,64},{64,7... | collective-permute-start | bytes 786440 | tf_op jit(solution)/shard_map/ppermute | solution.py:26
  62.9 52.3 %collective-permute-start.4 = (f32[64,8,128]{2,1,0:T(8,128)S(1)}, f32[64,8,128]{2,1,0:T(8,128)S(1)}, u32[]{:S(2)}, u32[]{:S(2)}) collective-permute-start(f32[64,8,128]{2,1,0:T(8,128)S(1)} %get-tuple-element.27), channel_id=1, source_target_pairs={{8,0},{16,8},{24,16},{32,24},{40,32},{48,40},{56,48},{64,56},{72,6... | collective-permute-start | bytes 786440 | tf_op jit(solution)/shard_map/ppermute | solution.py:27
  77.3 54.9 %collective-permute-start.7 = (f32[64,8,128]{2,1,0:T(8,128)S(1)}, f32[64,8,128]{2,1,0:T(8,128)S(1)}, u32[]{:S(2)}, u32[]{:S(2)}) collective-permute-start(f32[64,8,128]{2,1,0:T(8,128)S(1)} %get-tuple-element.30), channel_id=1, source_target_pairs={{0,8},{8,16},{16,24},{24,32},{32,40},{40,48},{48,56},{56,64},{64,7... | collective-permute-start | bytes 786440 | tf_op jit(solution)/shard_map/ppermute | solution.py:26
  82.2 51.3 %collective-permute-start.8 = (f32[64,8,128]{2,1,0:T(8,128)S(1)}, f32[64,8,128]{2,1,0:T(8,128)S(1)}, u32[]{:S(2)}, u32[]{:S(2)}) collective-permute-start(f32[64,8,128]{2,1,0:T(8,128)S(1)} %get-tuple-element.31), channel_id=1, source_target_pairs={{8,0},{16,8},{24,16},{32,24},{40,32},{48,40},{56,48},{64,56},{72,6... | collective-permute-start | bytes 786440 | tf_op jit(solution)/shard_map/ppermute | solution.py:27
  96.8 49.3 %collective-permute-start.5 = (f32[64,8,128]{2,1,0:T(8,128)S(1)}, f32[64,8,128]{2,1,0:T(8,128)S(1)}, u32[]{:S(2)}, u32[]{:S(2)}) collective-permute-start(f32[64,8,128]{2,1,0:T(8,128)S(1)} %get-tuple-element.28), channel_id=1, source_target_pairs={{0,8},{8,16},{16,24},{24,32},{32,40},{40,48},{48,56},{56,64},{64,7... | collective-permute-start | bytes 786440 | tf_op jit(solution)/shard_map/ppermute | solution.py:26
  113.9 32.2 %collective-permute-start.6 = (f32[64,8,128]{2,1,0:T(8,128)S(1)}, f32[64,8,128]{2,1,0:T(8,128)S(1)}, u32[]{:S(2)}, u32[]{:S(2)}) collective-permute-start(f32[64,8,128]{2,1,0:T(8,128)S(1)} %get-tuple-element.29), channel_id=1, source_target_pairs={{8,0},{16,8},{24,16},{32,24},{40,32},{48,40},{56,48},{64,56},{72,6... | collective-permute-start | bytes 786440 | tf_op jit(solution)/shard_map/ppermute | solution.py:27
  115.2 43.6 %collective-permute-start.1 = (f32[64,8,128]{2,1,0:T(8,128)S(1)}, f32[64,8,128]{2,1,0:T(8,128)S(1)}, u32[]{:S(2)}, u32[]{:S(2)}) collective-permute-start(f32[64,8,128]{2,1,0:T(8,128)S(1)} %get-tuple-element.24), channel_id=1, source_target_pairs={{0,8},{8,16},{16,24},{24,32},{32,40},{40,48},{48,56},{56,64},{64,7... | collective-permute-start | bytes 786440 | tf_op jit(solution)/shard_map/ppermute | solution.py:26
  132.2 26.6 %collective-permute-start.2 = (f32[64,8,128]{2,1,0:T(8,128)S(1)}, f32[64,8,128]{2,1,0:T(8,128)S(1)}, u32[]{:S(2)}, u32[]{:S(2)}) collective-permute-start(f32[64,8,128]{2,1,0:T(8,128)S(1)} %get-tuple-element.25), channel_id=1, source_target_pairs={{8,0},{16,8},{24,16},{32,24},{40,32},{48,40},{56,48},{64,56},{72,6... | collective-permute-start | bytes 786440 | tf_op jit(solution)/shard_map/ppermute | solution.py:27
where the time goes:
time: 336 us; the launch traced here: 334 us
  blocking collectives  162 us (48%)
  other arithmetic  109 us (32%)
  starting transfers between devices  32.7 us (10%)
  between operations  23.4 us (7%)
  waiting for transfers between devices  3.8 us (1%)
  local copies, waits for them, and re-layouts  3.62 us (1%)
    psum x1, blocking collectives, body(): sum_squares = lax.psum(jnp.sum(smoothed * smoothed, axis=(1, 2)), 'tile')  130 us
    add x4, other arithmetic, filter_along(): summed + kernel[offset] * lax.slice_in_dim(padded, offset, offset + lengt...  51.2 us
    reduce_sum x4, other arithmetic, body(): sum_squares = lax.psum(jnp.sum(smoothed * smoothed, axis=(1, 2)), 'tile')  50.4 us
    pmax x1, blocking collectives, body(): return lax.pmax(jnp.stack(peak_list), 'fblk')  31.9 us
    ppermute x4, starting transfers between devices, with_halo(): before = lax.ppermute(last, axis, up)  14.9 us
    all_to_all x1, starting transfers between devices, body(): lax.all_to_all(planes, 'tile', split_axis=1, concat_axis=0, tiled=True)  10.7 us
  transfers between devices with their start and end apart: 10, of which 1 were waited for; matrix products, arithmetic and copies ran while one was open for 26% of the time, Pallas kernels for 0%

commit v1 on v0

--- a/solution.py
+++ b/solution.py
@@ -78,7 +78,9 @@
         horizontal = filter_along(pad_along(spectral, 2), kernel, 2)
         bordered = with_halo(horizontal, (("tile", 1),), RAD)
         smoothed = filter_along(bordered, kernel, 1)
-        sum_squares = lax.psum(jnp.sum(smoothed * smoothed, axis=(1, 2)), "tile")
+        sum_squares = jnp.sum(
+            lax.all_gather(jnp.sum(smoothed * smoothed, axis=(1, 2)), "tile"), axis=0
+        )
         peak_list.append(channel_peak(smoothed, sum_squares, cells))
     return lax.pmax(jnp.stack(peak_list), "fblk")
 

time: 336 us -> 426 us (1.27)
  the two profiles are of different devices: /device:TPU:64 before, /device:TPU:2 now
where the time goes in v1:
time: 426 us; the launch traced here: 424 us
  waiting for transfers between devices  184 us (43%)
  other arithmetic  115 us (27%)
  starting transfers between devices  42.8 us (10%)
  between operations  37.4 us (9%)
  blocking collectives  31.5 us (7%)
  local copies, waits for them, and re-layouts  12.6 us (3%)
    unnamed x2, waiting for transfers between devices  180 us
    reduce_sum x4, other arithmetic, body(): jnp.sum(smoothed * smoothed, axis=(1, 2))  56.8 us
    add x4, other arithmetic, filter_along(): summed + kernel[offset] * lax.slice_in_dim(padded, offset, offset + lengt...  51.3 us
    pmax x1, blocking collectives, body(): return lax.pmax(jnp.stack(peak_list), 'fblk')  31.5 us
    ppermute x4, starting transfers between devices, with_halo(): after = lax.ppermute(leading, axis, down)  23 us
    all_to_all x1, starting transfers between devices, body(): lax.all_to_all(planes, 'tile', split_axis=1, concat_axis=0, tiled=True)  10.7 us
  transfers between devices with their start and end apart: 11, of which 2 were waited for; matrix products, arithmetic and copies ran while one was open for 22% of the time, Pallas kernels for 0%

profile of v1, /device:TPU:2, one launch (start us, length us, event | category | flops | bytes accessed | tf_op | source)
XLA Modules:
  0.0 423.6 jit_solution(8029322721546994997)
XLA Ops:
  6.5 10.7 %all-to-all-start = ((f32[1,1024,128]{2,0,1:T(1,128)}), f32[1,1024,128]{2,0,1:T(1,128)S(1)}, u32[]{:S(2)}, u32[]{:S(2)}) async-start(f32[1,1024,128]{2,0,1:T(1,128)} %bitcast.112), calls=%async_computation | async-start | bytes 1048576 | tf_op jit(solution)/shard_map/all_to_all | solution.py:69
  41.6 1.3 dynamic-slice
  50.8 1.3 collective-permute-start
  52.8 4.5 %collective-permute-done = f32[7,16,128]{2,1,0:T(8,128)S(1)} collective-permute-done((f32[7,16,128]{2,1,0:T(8,128)S(1)}, f32[7,16,128]{2,1,0:T(8,128)S(1)}, u32[]{:S(2)}, u32[]{:S(2)}) %collective-permute-start) | collective-permute-done | bytes 57376 | tf_op jit(solution)/shard_map/ppermute | solution.py:16
  58.0 12.8 %fusion.230 = f32[64,16,128]{2,1,0:T(8,128)S(1)} fusion(f32[64,16,128]{2,1,0:T(8,128)S(1)} %multiply_add_fusion.2, f32[]{:T(128)} %bitcast.54, f32[]{:T(128)} %bitcast.53, f32[]{:T(128)} %bitcast.52, f32[]{:T(128)} %bitcast.51, f32[]{:T(128)} %bitcast.50, f32[]{:T(128)} %bitcast.49, f32[]{:T(128)} %bitcast.48, f32[]{:T(128)} %bitcast.47, f32[]{:T(128)} %bitcast.46, ...), kind=kLoop, calls=%fused_computation.418 | loop fusion | flops 4325376 | bytes 1048644 | tf_op jit(solution)/shard_map/add | solution.py:48
  70.8 1.9 collective-permute-start.3
  72.8 5.8 %collective-permute-start.4 = (f32[64,8,128]{2,1,0:T(8,128)S(1)}, f32[64,8,128]{2,1,0:T(8,128)S(1)}, u32[]{:S(2)}, u32[]{:S(2)}) collective-permute-start(f32[64,8,128]{2,1,0:T(8,128)S(1)} %get-tuple-element.27), channel_id=1, source_target_pairs={{8,0},{16,8},{24,16},{32,24},{40,32},{48,40},{56,48},{64,56},{72,6... | collective-permute-start | bytes 786440 | tf_op jit(solution)/shard_map/ppermute | solution.py:27
  78.8 12.8 %fusion.294 = f32[64,16,128]{2,1,0:T(8,128)S(1)} fusion(f32[64,16,128]{2,1,0:T(8,128)S(1)} %multiply_add_fusion, f32[]{:T(128)} %bitcast.106, f32[]{:T(128)} %bitcast.105, f32[]{:T(128)} %bitcast.104, f32[]{:T(128)} %bitcast.103, f32[]{:T(128)} %bitcast.102, f32[]{:T(128)} %bitcast.101, f32[]{:T(128)} %bitcast.100, f32[]{:T(128)} %bitcast.99, f32[]{:T(128)} %bitcast.98, ...), kind=kLoop, calls=%fused_computation.482 | loop fusion | flops 4325376 | bytes 1048644 | tf_op jit(solution)/shard_map/add | solution.py:48
  91.6 0.8 fusion.335
  92.5 1.9 collective-permute-start.7
  94.4 5.8 %collective-permute-start.8 = (f32[64,8,128]{2,1,0:T(8,128)}, f32[64,8,128]{2,1,0:T(8,128)}, u32[]{:S(2)}, u32[]{:S(2)}) collective-permute-start(f32[64,8,128]{2,1,0:T(8,128)} %get-tuple-element.31), channel_id=1, source_target_pairs={{8,0},{16,8},{24,16},{32,24},{40,32},{48,40},{56,48},{64,56},{72,6... | collective-permute-start | bytes 786440 | tf_op jit(solution)/shard_map/ppermute | solution.py:27
  100.4 12.7 %fusion.262 = f32[64,16,128]{2,1,0:T(8,128)S(1)} fusion(f32[64,16,128]{2,1,0:T(8,128)S(1)} %multiply_add_fusion.1, f32[]{:T(128)} %bitcast.80, f32[]{:T(128)} %bitcast.79, f32[]{:T(128)} %bitcast.78, f32[]{:T(128)} %bitcast.77, f32[]{:T(128)} %bitcast.76, f32[]{:T(128)} %bitcast.75, f32[]{:T(128)} %bitcast.74, f32[]{:T(128)} %bitcast.73, f32[]{:T(128)} %bitcast.72, ...), kind=kLoop, calls=%fused_computation.450 | loop fusion | flops 4325376 | bytes 1048644 | tf_op jit(solution)/shard_map/add | solution.py:48
  113.1 0.9 fusion.334
  114.0 1.9 collective-permute-start.5
  115.9 12.9 %fusion.198 = f32[64,16,128]{2,1,0:T(8,128)S(1)} fusion(f32[64,16,128]{2,1,0:T(8,128)S(1)} %get-tuple-element.11, f32[]{:T(128)} %bitcast.27, f32[]{:T(128)} %bitcast.26, f32[]{:T(128)} %bitcast.25, f32[]{:T(128)} %bitcast.24, f32[]{:T(128)} %bitcast.23, f32[]{:T(128)} %bitcast.22, f32[]{:T(128)} %bitcast.21, f32[]{:T(128)} %bitcast.20, f32[]{:T(128)} %bitcast.19, ...), kind=kLoop, calls=%fused_computation.386 | loop fusion | flops 4325376 | bytes 1048644 | tf_op jit(solution)/shard_map/add | solution.py:48
  129.6 5.7 %collective-permute-start.6 = (f32[64,8,128]{2,1,0:T(8,128)}, f32[64,8,128]{2,1,0:T(8,128)}, u32[]{:S(2)}, u32[]{:S(2)}) collective-permute-start(f32[64,8,128]{2,1,0:T(8,128)} %get-tuple-element.29), channel_id=1, source_target_pairs={{8,0},{16,8},{24,16},{32,24},{40,32},{48,40},{56,48},{64,56},{72,6... | collective-permute-start | bytes 786440 | tf_op jit(solution)/shard_map/ppermute | solution.py:27
  135.3 2.1 collective-permute-start.1
  137.4 12.6 %multiply_reduce_fusion.2 = (f32[64]{0:T(128)S(1)}, f32[64,16,128]{2,1,0:T(8,128)S(1)}) fusion(f32[64,8,128]{2,1,0:T(8,128)S(1)} %collective-permute-done.4, f32[64,16,128]{2,1,0:T(8,128)S(1)} %fusion.230, f32[]{:T(128)} %bitcast.54, f32[]{:T(128)} %bitcast.53, f32[]{:T(128)} %bitcast.52, f32[]{:T(128)} %bitcast.51, f32[]{:T(128)} %bitcast.50, f32[]{:T(128)} %bitcast.49, ...), kind=kLoop, calls=%fused_computation.519 | loop fusion | flops 6684608 | bytes 1573188 | tf_op jit(solution)/shard_map/reduce_sum | solution.py:82
  150.3 5.8 %collective-permute-start.2 = (f32[64,8,128]{2,1,0:T(8,128)S(1)}, f32[64,8,128]{2,1,0:T(8,128)}, u32[]{:S(2)}, u32[]{:S(2)}) collective-permute-start(f32[64,8,128]{2,1,0:T(8,128)S(1)} %get-tuple-element.25), channel_id=1, source_target_pairs={{8,0},{16,8},{24,16},{32,24},{40,32},{48,40},{56,48},{64,56},{72,6... | collective-permute-start | bytes 786440 | tf_op jit(solution)/shard_map/ppermute | solution.py:27
  156.1 15.3 %multiply_reduce_fusion = (f32[64]{0:T(128)S(1)}, f32[64,16,128]{2,1,0:T(8,128)S(1)}) fusion(f32[64,8,128]{2,1,0:T(8,128)} %collective-permute-done.8, f32[64,16,128]{2,1,0:T(8,128)S(1)} %fusion.294, f32[]{:T(128)} %bitcast.106, f32[]{:T(128)} %bitcast.105, f32[]{:T(128)} %bitcast.104, f32[]{:T(128)} %bitcast.103, f32[]{:T(128)} %bitcast.102, f32[]{:T(128)} %bitcast.101, ...), kind=kLoop, calls=%fused_computation.515 | loop fusion | flops 6684608 | bytes 1573188 | tf_op jit(solution)/shard_map/reduce_sum | solution.py:82
  171.7 14.3 %multiply_reduce_fusion.1 = (f32[64]{0:T(128)S(1)}, f32[64,16,128]{2,1,0:T(8,128)S(1)}) fusion(f32[64,8,128]{2,1,0:T(8,128)} %collective-permute-done.6, f32[64,16,128]{2,1,0:T(8,128)S(1)} %fusion.262, f32[]{:T(128)} %bitcast.80, f32[]{:T(128)} %bitcast.79, f32[]{:T(128)} %bitcast.78, f32[]{:T(128)} %bitcast.77, f32[]{:T(128)} %bitcast.76, f32[]{:T(128)} %bitcast.75, ...), kind=kLoop, calls=%fused_computation.517 | loop fusion | flops 6684608 | bytes 1573188 | tf_op jit(solution)/shard_map/reduce_sum | solution.py:82
  186.3 14.6 %multiply_reduce_fusion.3 = (f32[64]{0:T(128)S(1)}, f32[64,16,128]{2,1,0:T(8,128)S(1)}) fusion(f32[64,8,128]{2,1,0:T(8,128)} %collective-permute-done.2, f32[64,16,128]{2,1,0:T(8,128)S(1)} %fusion.198, f32[]{:T(128)} %bitcast.27, f32[]{:T(128)} %bitcast.26, f32[]{:T(128)} %bitcast.25, f32[]{:T(128)} %bitcast.24, f32[]{:T(128)} %bitcast.23, f32[]{:T(128)} %bitcast.22, ...), kind=kLoop, calls=%fused_computation.521 | loop fusion | flops 6684608 | bytes 1573188 | tf_op jit(solution)/shard_map/reduce_sum | solution.py:82
  201.9 179.6 %all-reduce.11.cloned.1.call-done = (f32[4096]{0:T(1024)}, f32[4096]{0:T(1024)}, f32[4096]{0:T(1024)}, f32[4096]{0:T(1024)}) async-done(((f32[4096]{0:T(1024)}, f32[4096]{0:T(1024)}, f32[4096]{0:T(1024)}, f32[4096]{0:T(1024)}), (f32[4096]{0:T(1024)}, f32[4096]{0:T(1024)}, f32[4096]{0:T(1024)}, f32[4096]{0:T(1024)})) %all-reduce.11.cloned.1.call-update) | async-done | bytes 65552
  385.3 31.5 %pmax.7 = f32[4,16,128]{2,1,0:T(8,128)} all-reduce(f32[4,16,128]{2,1,0:T(8,128)S(1)} %pad_maximum_fusion.9), channel_id=1, replica_groups=mesh['tile'=64,'fblk'=8] {'fblk'}, use_global_device_ids=true, to_apply=%region_16.17 | all-reduce | flops 8192 | bytes 65536 | tf_op jit(solution)/shard_map/pmax | solution.py:85
  (74 shorter events, 16.8 us)
Async XLA Ops:
  6.5 44.3 %all-to-all-start = ((f32[1,1024,128]{2,0,1:T(1,128)}), f32[1,1024,128]{2,0,1:T(1,128)S(1)}, u32[]{:S(2)}, u32[]{:S(2)}) async-start(f32[1,1024,128]{2,0,1:T(1,128)} %bitcast.112), calls=%async_computation | async-start | bytes 1048576 | tf_op jit(solution)/shard_map/all_to_all | solution.py:69
  17.2 364.3 %all-reduce.11.cloned.1.call-start = ((), (), s32[]{:S(2)}) async-start(), calls=%async_computation.1 | async-start | bytes 131072
  17.3 0.7 copy-start.8
  50.8 6.5 %collective-permute-start = (f32[7,16,128]{2,1,0:T(8,128)S(1)}, f32[7,16,128]{2,1,0:T(8,128)S(1)}, u32[]{:S(2)}, u32[]{:S(2)}) collective-permute-start(f32[7,16,128]{2,1,0:T(8,128)S(1)} %bitcast.113), channel_id=1, source_target_pairs={{1,0},{2,1},{3,2},{4,3},{5,4},{6,5},{7,6},{9,8},{10,9},{11,10},{12... | collective-permute-start | bytes 172040 | tf_op jit(solution)/shard_map/ppermute | solution.py:16
  70.8 58.7 %collective-permute-start.3 = (f32[64,8,128]{2,1,0:T(8,128)S(1)}, f32[64,8,128]{2,1,0:T(8,128)S(1)}, u32[]{:S(2)}, u32[]{:S(2)}) collective-permute-start(f32[64,8,128]{2,1,0:T(8,128)S(1)} %get-tuple-element.26), channel_id=1, source_target_pairs={{0,8},{8,16},{16,24},{24,32},{32,40},{40,48},{48,56},{56,64},{64,7... | collective-permute-start | bytes 786440 | tf_op jit(solution)/shard_map/ppermute | solution.py:26
  72.8 62.5 %collective-permute-start.4 = (f32[64,8,128]{2,1,0:T(8,128)S(1)}, f32[64,8,128]{2,1,0:T(8,128)S(1)}, u32[]{:S(2)}, u32[]{:S(2)}) collective-permute-start(f32[64,8,128]{2,1,0:T(8,128)S(1)} %get-tuple-element.27), channel_id=1, source_target_pairs={{8,0},{16,8},{24,16},{32,24},{40,32},{48,40},{56,48},{64,56},{72,6... | collective-permute-start | bytes 786440 | tf_op jit(solution)/shard_map/ppermute | solution.py:27
  92.5 57.9 %collective-permute-start.7 = (f32[64,8,128]{2,1,0:T(8,128)}, f32[64,8,128]{2,1,0:T(8,128)S(1)}, u32[]{:S(2)}, u32[]{:S(2)}) collective-permute-start(f32[64,8,128]{2,1,0:T(8,128)} %get-tuple-element.30), channel_id=1, source_target_pairs={{0,8},{8,16},{16,24},{24,32},{32,40},{40,48},{48,56},{56,64},{64,7... | collective-permute-start | bytes 786440 | tf_op jit(solution)/shard_map/ppermute | solution.py:26
  94.4 61.7 %collective-permute-start.8 = (f32[64,8,128]{2,1,0:T(8,128)}, f32[64,8,128]{2,1,0:T(8,128)}, u32[]{:S(2)}, u32[]{:S(2)}) collective-permute-start(f32[64,8,128]{2,1,0:T(8,128)} %get-tuple-element.31), channel_id=1, source_target_pairs={{8,0},{16,8},{24,16},{32,24},{40,32},{48,40},{56,48},{64,56},{72,6... | collective-permute-start | bytes 786440 | tf_op jit(solution)/shard_map/ppermute | solution.py:27
  114.0 57.7 %collective-permute-start.5 = (f32[64,8,128]{2,1,0:T(8,128)}, f32[64,8,128]{2,1,0:T(8,128)S(1)}, u32[]{:S(2)}, u32[]{:S(2)}) collective-permute-start(f32[64,8,128]{2,1,0:T(8,128)} %get-tuple-element.28), channel_id=1, source_target_pairs={{0,8},{8,16},{16,24},{24,32},{32,40},{40,48},{48,56},{56,64},{64,7... | collective-permute-start | bytes 786440 | tf_op jit(solution)/shard_map/ppermute | solution.py:26
  129.6 42.2 %collective-permute-start.6 = (f32[64,8,128]{2,1,0:T(8,128)}, f32[64,8,128]{2,1,0:T(8,128)}, u32[]{:S(2)}, u32[]{:S(2)}) collective-permute-start(f32[64,8,128]{2,1,0:T(8,128)} %get-tuple-element.29), channel_id=1, source_target_pairs={{8,0},{16,8},{24,16},{32,24},{40,32},{48,40},{56,48},{64,56},{72,6... | collective-permute-start | bytes 786440 | tf_op jit(solution)/shard_map/ppermute | solution.py:27
  135.3 51.0 %collective-permute-start.1 = (f32[64,8,128]{2,1,0:T(8,128)}, f32[64,8,128]{2,1,0:T(8,128)S(1)}, u32[]{:S(2)}, u32[]{:S(2)}) collective-permute-start(f32[64,8,128]{2,1,0:T(8,128)} %get-tuple-element.24), channel_id=1, source_target_pairs={{0,8},{8,16},{16,24},{24,32},{32,40},{40,48},{48,56},{56,64},{64,7... | collective-permute-start | bytes 786440 | tf_op jit(solution)/shard_map/ppermute | solution.py:26
  150.3 21.1 %copy-start.2 = (f32[4096]{0:T(1024)}, f32[4096]{0:T(1024)S(1)}, u32[]{:S(2)}) copy-start(f32[4096]{0:T(1024)S(1)} %dynamic-update-slice.1) | copy-start | bytes 49156
  150.3 5.8 %copy-start = (f32[64,8,128]{2,1,0:T(8,128)}, f32[64,8,128]{2,1,0:T(8,128)S(1)}, u32[]{:S(2)}) copy-start(f32[64,8,128]{2,1,0:T(8,128)S(1)} %collective-permute-done.7) | copy-start | bytes 786436
  150.3 36.0 %collective-permute-start.2 = (f32[64,8,128]{2,1,0:T(8,128)S(1)}, f32[64,8,128]{2,1,0:T(8,128)}, u32[]{:S(2)}, u32[]{:S(2)}) collective-permute-start(f32[64,8,128]{2,1,0:T(8,128)S(1)} %get-tuple-element.25), channel_id=1, source_target_pairs={{8,0},{16,8},{24,16},{32,24},{40,32},{48,40},{56,48},{64,56},{72,6... | collective-permute-start | bytes 786440 | tf_op jit(solution)/shard_map/ppermute | solution.py:27
  171.7 14.3 %copy-start.3 = (f32[4096]{0:T(1024)}, f32[4096]{0:T(1024)S(1)}, u32[]{:S(2)}) copy-start(f32[4096]{0:T(1024)S(1)} %dynamic-update-slice.3) | copy-start | bytes 49156
  186.3 14.6 %copy-start.4 = (f32[4096]{0:T(1024)}, f32[4096]{0:T(1024)S(1)}, u32[]{:S(2)}) copy-start(f32[4096]{0:T(1024)S(1)} %dynamic-update-slice.2) | copy-start | bytes 49156
  201.3 0.6 copy-start.1
  382.3 0.7 copy-start.7
  383.1 0.7 copy-start.6
  383.9 0.7 copy-start.5
Sparse Core Ops, SparseCore 0:
  202.0 179.4 all-reduce.10
